TPU v7x, 128 devices: a whole 4x4x4 slice. The times are simulated.
128 devices in a mesh: tm: 16 (over x, z), batch: 8 (over y, core).
Axes of the slice: x: 4, y: 4, z: 4, core: 2. Of those that a mesh axis runs over, the one named last changes fastest.
Arguments:
- state: float32 [16, 8, 256, 1152], P('tm', 'batch'), may hold values from -6 to 6
- noise_draws: bfloat16 [2, 16, 8, 256, 1152], P(None, 'tm', 'batch'), may hold values from -6 to 6
- class_vec: float32 [8, 1152], P('batch'), may hold values from -6 to 6
- window_start: int32 [8], P('batch'), may hold values from 0 to 977
- advance: int32 [8], P('batch'), may hold values from 1 to 7
- step_dt: float32 [1000], replicated, may hold values from 0.05 to 0.2
- step_sigma: float32 [1000], replicated, may hold values from 0.05 to 0.2
- w_ada: bfloat16 [1152, 3456], replicated, may hold values from -0.1875 to 0.1875
- w_up: bfloat16 [4608, 1152], P(('tm', 'batch')), may hold values from -0.1875 to 0.1875
- w_down: bfloat16 [4608, 1152], P(('tm', 'batch')), may hold values from -0.09375 to 0.09375
Outputs:
- window_out: float32 [16, 8, 256, 1152], P('tm', 'batch')
All inputs are finite; a program needn't handle non-finite values.
Results may differ from a plain program's by a relative error of at most 0.0037.
Values may be sent and summed in bfloat16 or wider, within the bound.
No kernel may reach another device: no remote copies, remote signals or barrier semaphores. Data moves between devices by JAX's collectives and lax.ppermute only.
A program may use at most 128 MiB of HBM per device.

v0:
```python
import math
import jax
import jax.numpy as jnp
from jax import lax
from jax.sharding import PartitionSpec as P

SLIDE_BITS = 3
EPSILON = 1e-06


def spread_2(shard, axis, root):
    mine = lax.axis_index(axis) == root
    return lax.psum(jnp.where(mine, shard, jnp.zeros_like(shard)), axis)


def carried_in(part, axis, combine, identity):
    place = lax.axis_index(axis)
    gathered = lax.all_gather(part, axis)
    state = jnp.zeros_like(part) + jnp.asarray(identity, part.dtype)

    def one(turn, state):
        return combine(state, lax.dynamic_index_in_dim(gathered, turn, 0, False))

    return lax.fori_loop(0, place, one, state)


def from_behind(shard, axis, by):
    peers = lax.axis_size(axis)
    pairs = [(i, i + by) for i in range(peers) if 0 <= i + by < peers]
    return lax.ppermute(shard, axis, pairs)


def time_embed(steps_now, half_width):
    frequency = jnp.exp(-math.log(10000.0) * jnp.arange(half_width, dtype=jnp.float32) / half_width)
    angles = steps_now.astype(jnp.float32)[:, None] * frequency[None, :]
    return jnp.concatenate([jnp.cos(angles), jnp.sin(angles)], axis=1)


def dense_pair(hidden_rows, up_rows, down_rows):
    before = lax.dot_general(
        hidden_rows, up_rows, (((1,), (1,)), ((), ())), preferred_element_type=jnp.float32
    )
    activated = jax.nn.gelu(before, approximate=True).astype(jnp.bfloat16)
    return jnp.dot(activated, down_rows, preferred_element_type=jnp.float32)


def combine_sum(earlier, later):
    return earlier + later


def increment(current, noise_now, steps_now, class_vec, step_dt, step_sigma, w_ada, mlp_apply):
    images, tokens, channels = current.shape
    step_table = lax.iota(jnp.int32, step_dt.shape[0])
    onehot = (steps_now[:, None] == step_table[None, :]).astype(jnp.float32)
    step_size = jnp.sum(onehot * step_dt[None, :], axis=1)
    spread = jnp.sum(onehot * step_sigma[None, :], axis=1)
    condition = jax.nn.silu(time_embed(steps_now, channels // 2) + class_vec).astype(jnp.bfloat16)
    modulation = jnp.dot(condition, w_ada, preferred_element_type=jnp.float32)
    shift_by = modulation[:, :channels]
    scale_by = modulation[:, channels : 2 * channels]
    gate_by = modulation[:, 2 * channels :]
    mean_val = jnp.mean(current, axis=2, keepdims=True)
    centred = current - mean_val
    var_val = jnp.mean(centred * centred, axis=2, keepdims=True)
    normed = centred * lax.rsqrt(var_val + EPSILON)
    hidden_in = (normed * (1.0 + scale_by[:, None, :]) + shift_by[:, None, :]).astype(jnp.bfloat16)
    mlp_out = mlp_apply(hidden_in.reshape(images * tokens, channels)).reshape(
        images, tokens, channels
    )
    drift = gate_by[:, None, :] * mlp_out - current
    return step_size[:, None, None] * drift + spread[:, None, None] * noise_now.astype(jnp.float32)


def per_device(
    state, noise_draws, class_vec, window_start, advance, step_dt, step_sigma, w_ada, w_up, w_down
):
    window_size = lax.axis_size("tm")
    position = lax.axis_index("tm")
    up_whole, down_whole = (
        lax.all_gather(w_up, ("tm", "batch"), axis=0, tiled=True),
        lax.all_gather(w_down, ("tm", "batch"), axis=0, tiled=True),
    )

    def mlp_apply(hidden_rows):
        return dense_pair(hidden_rows, up_whole, down_whole)

    def sweep(current, noise_now, starts):
        steps_now = starts + position
        step_inc = increment(
            current, noise_now, steps_now, class_vec, step_dt, step_sigma, w_ada, mlp_apply
        )
        base_rows = spread_2(current, "tm", 0)
        prefix = carried_in(step_inc, "tm", combine_sum, jnp.zeros_like(step_inc))
        updated = base_rows + prefix
        return (updated, step_inc)

    updated, step_inc = sweep(state[0], noise_draws[0, 0], window_start)
    end_rows = updated + step_inc
    tail_rows = jnp.where(position == window_size - 1, end_rows, jnp.zeros_like(end_rows))
    moved = updated
    for section_bit in range(SLIDE_BITS):
        distance = 1 << section_bit
        arrived, arrived_tail = from_behind((moved, tail_rows), "tm", -distance)
        taken = advance >> section_bit & 1 == 1
        outside = position + distance >= window_size
        incoming = jnp.where(outside, tail_rows, arrived)
        moved = jnp.where(taken[:, None, None], incoming, moved)
        tail_rows = jnp.where(position >= window_size - distance, tail_rows, arrived_tail)
    final_rows, leftover = sweep(moved, noise_draws[1, 0], window_start + advance)
    return final_rows[None]


def solution(mesh):
    in_specs = (
        P("tm", "batch", None, None),
        P(None, "tm", "batch", None, None),
        P("batch", None),
        P("batch"),
        P("batch"),
        P(),
        P(),
        P(),
        P(("tm", "batch"), None),
        P(("tm", "batch"), None),
    )
    out_specs = P("tm", "batch", None, None)
    return jax.shard_map(
        per_device, mesh=mesh, in_specs=in_specs, out_specs=out_specs, check_vma=False
    )
```

profile of v0, /device:TPU:0, one launch (start us, length us, event | category | flops | bytes accessed | tf_op | source)
XLA Modules:
  0.0 791.6 jit_solution(7158159004411722302)
XLA Ops:
  6.5 0.0 copy-start.9
  6.5 0.0 copy-start.6
  6.5 0.0 all-gather.15.cloned.1.call-start
  6.5 0.7 all-gather.15.cloned.1.call-update
  7.3 0.0 all-gather.13.cloned.1.call-start
  7.3 0.7 all-gather.13.cloned.1.call-update
  8.0 0.0 all-gather.9.cloned.1.call-start
  9.4 1.4 reduce_sum.73
  10.8 0.1 fusion.87
  10.9 0.0 copy-done.8
  10.9 0.0 copy-done.9
  10.9 0.7 select_reduce_fusion
  11.6 0.0 copy-done.6
  11.6 4.5 fusion.73
  16.2 0.0 copy-done.1
  16.2 1.2 fusion.39
  17.4 68.0 %all-gather.15.cloned.1.call-done = bf16[128,36,1152]{2,1,0:T(8,128)(2,1)} async-done(((bf16[1,36,1152]{2,1,0:T(8,128)(2,1)}), bf16[128,36,1152]{2,1,0:T(8,128)(2,1)}) %all-gather.15.cloned.1.call-update) | async-done | bytes 10616848 | tf_op jit(solution)/shard_map/all_gather | solution.py:81
  85.3 16.3 %reshape.304 = bf16[4608,1152]{1,0:T(8,128)(2,1)} reshape(bf16[128,36,1152]{2,1,0:T(8,128)(2,1)} %all-gather.15.cloned.1.call-done) | data formatting | bytes 21233664
  101.6 58.2 %all-gather.13.cloned.1.call-done = bf16[128,36,1152]{2,1,0:T(8,128)(2,1)} async-done(((bf16[1,36,1152]{2,1,0:T(8,128)(2,1)}), bf16[128,36,1152]{2,1,0:T(8,128)(2,1)}) %all-gather.13.cloned.1.call-update) | async-done | bytes 10616848 | tf_op jit(solution)/shard_map/all_gather | solution.py:80
  159.9 16.3 %reshape.302 = bf16[4608,1152]{1,0:T(8,128)(2,1)} reshape(bf16[128,36,1152]{2,1,0:T(8,128)(2,1)} %all-gather.13.cloned.1.call-done) | data formatting | bytes 21233664
  176.2 0.0 copy-done.10
  176.2 15.8 %fusion.18 = f32[256,1152]{1,0:T(8,128)} fusion(bf16[4608,1152]{1,0:T(8,128)(2,1)} %reshape.304, f32[1,1,256,1152]{3,2,1,0:T(8,128)S(1)} %copy-done.1, bf16[4608,1152]{1,0:T(8,128)(2,1)} %reshape.302, bf16[2,1,1,256,1152]{4,3,2,1,0:T(8,128)(2,1)S(1)} %copy-done.10, f32[]{:T(128)} %get-tuple-element.86, f32[1152]{0:T(1024)S(1)} %get-tuple-element.82, ...), kind=kOutput, calls=%fused_computation.24 | convolution fusion | flops 5449678848 | bytes 25389064 | tf_op jit(solution)/shard_map/dot_general | solution.py:44
  192.0 0.0 all-gather.9.cloned.1.call-update
  192.0 0.0 all-reduce.3.cloned.1.call-start
  192.1 0.5 all-reduce.3.cloned.1.call-update
  192.6 0.0 all-gather.11.cloned.1.call-start
  192.6 120.7 %all-gather.9.cloned.1.call-done = f32[4096,1152]{1,0:T(8,128)} async-done(((f32[256,1152]{1,0:T(8,128)}), f32[4096,1152]{1,0:T(8,128)}) %all-gather.9.cloned.1.call-update) | async-done | bytes 18874384 | tf_op jit(solution)/shard_map/all_gather | solution.py:18
  313.3 0.1 broadcast.231.clone
  313.4 89.8 %all-reduce.3.cloned.1.call-done = f32[1,256,1152]{2,1,0:T(8,128)} async-done(((f32[1,256,1152]{2,1,0:T(8,128)}), f32[1,256,1152]{2,1,0:T(8,128)}) %all-reduce.3.cloned.1.call-update) | async-done | bytes 1179664 | tf_op jit(solution)/shard_map/psum | solution.py:13
  403.2 1.5 add.160
  404.7 1.3 collective-permute-start.2
  406.0 26.8 %collective-permute-done.2 = f32[1,256,1152]{2,1,0:T(8,128)S(1)} collective-permute-done((f32[1,256,1152]{2,1,0:T(8,128)S(1)}, f32[1,256,1152]{2,1,0:T(8,128)S(1)}, u32[]{:S(2)}, u32[]{:S(2)}) %collective-permute-start.2) | collective-permute-done | bytes 1179680 | tf_op jit(solution)/shard_map/ppermute | solution.py:30
  432.8 1.0 copy-done.2
  433.8 0.0 copy-done
  433.9 2.5 select_select_fusion.2
  436.3 1.3 collective-permute-start.3
  437.6 1.3 collective-permute-start
  438.9 26.1 %collective-permute-done.3 = f32[1,256,1152]{2,1,0:T(8,128)S(1)} collective-permute-done((f32[1,256,1152]{2,1,0:T(8,128)S(1)}, f32[1,256,1152]{2,1,0:T(8,128)S(1)}, u32[]{:S(2)}, u32[]{:S(2)}) %collective-permute-start.3) | collective-permute-done | bytes 1179680 | tf_op jit(solution)/shard_map/ppermute | solution.py:30
  465.0 25.3 %collective-permute-done = f32[1,256,1152]{2,1,0:T(8,128)S(1)} collective-permute-done((f32[1,256,1152]{2,1,0:T(8,128)}, f32[1,256,1152]{2,1,0:T(8,128)S(1)}, u32[]{:S(2)}, u32[]{:S(2)}) %collective-permute-start) | collective-permute-done | bytes 1179680 | tf_op jit(solution)/shard_map/ppermute | solution.py:30
  490.3 0.0 copy-done.4
  490.3 1.0 copy-done.5
  491.4 1.9 select_select_fusion.1
  493.2 1.3 collective-permute-start.4
  494.5 1.5 collective-permute-start.1
  496.0 0.1 fusion.85
  496.1 4.4 fusion.71
  500.5 0.6 slice_reduce_fusion.1
  501.2 22.9 %collective-permute-done.4 = f32[1,256,1152]{2,1,0:T(8,128)S(1)} collective-permute-done((f32[1,256,1152]{2,1,0:T(8,128)S(1)}, f32[1,256,1152]{2,1,0:T(8,128)S(1)}, u32[]{:S(2)}, u32[]{:S(2)}) %collective-permute-start.4) | collective-permute-done | bytes 1179680 | tf_op jit(solution)/shard_map/ppermute | solution.py:30
  524.1 0.7 collective-permute-done.1
  524.8 0.3 copy-done.3
  525.1 1.9 fusion.101
  527.0 0.0 copy-start.7
  527.0 0.0 copy-start.11
  527.0 1.2 multiply_reduce_fusion
  528.2 0.0 copy-done.7
  528.2 0.4 copy-done.11
  528.6 15.9 %fusion.22 = f32[1,256,1152]{2,1,0:T(8,128)} fusion(f32[1,256,1152]{2,1,0:T(8,128)S(1)} %get-tuple-element.104, bf16[4608,1152]{1,0:T(8,128)(2,1)} %reshape.304, bf16[4608,1152]{1,0:T(8,128)(2,1)} %reshape.302, bf16[2,1,1,256,1152]{4,3,2,1,0:T(8,128)(2,1)S(1)} %copy-done.11, f32[]{:T(128)} %get-tuple-element.85, f32[1152]{0:T(1024)S(1)} %copy-done.7, ...), kind=kOutput, calls=%fused_computation.28 | convolution fusion | flops 5449678848 | bytes 25389064 | tf_op jit(solution)/shard_map/dot_general | solution.py:44
  544.5 0.0 all-gather.11.cloned.1.call-update
  544.5 0.0 all-reduce.5.cloned.1.call-start
  544.6 0.5 all-reduce.5.cloned.1.call-update
  545.1 147.3 %all-gather.11.cloned.1.call-done = f32[16,256,1152]{2,1,0:T(8,128)} async-done(((f32[1,256,1152]{2,1,0:T(8,128)}), f32[16,256,1152]{2,1,0:T(8,128)}) %all-gather.11.cloned.1.call-update) | async-done | bytes 18874384 | tf_op jit(solution)/shard_map/all_gather | solution.py:18
  692.4 0.1 broadcast.231
  692.5 89.8 %all-reduce.5.cloned.1.call-done = f32[1,256,1152]{2,1,0:T(8,128)} async-done(((f32[1,256,1152]{2,1,0:T(8,128)}), f32[1,256,1152]{2,1,0:T(8,128)}) %all-reduce.5.cloned.1.call-update) | async-done | bytes 1179664 | tf_op jit(solution)/shard_map/psum | solution.py:13
  782.3 2.4 add_bitcast_fusion
  (15 shorter events, 0.1 us)
Async XLA Ops:
  6.5 4.3 copy-start.8
  6.5 4.3 copy-start.9
  6.5 5.0 copy-start.6
  6.5 78.8 %all-gather.15.cloned.1.call-start = ((), (), s32[]{:S(2)}) async-start(), calls=%async_computation.5 | async-start | bytes 11888640 | tf_op jit(solution)/shard_map/all_gather | solution.py:81
  7.3 152.6 %all-gather.13.cloned.1.call-start = ((), (), s32[]{:S(2)}) async-start(), calls=%async_computation.4 | async-start | bytes 11888640 | tf_op jit(solution)/shard_map/all_gather | solution.py:80
  8.0 305.3 %all-gather.9.cloned.1.call-start = ((), (), s32[]{:S(2)}) async-start(), calls=%async_computation.2 | async-start | bytes 20054016 | tf_op jit(solution)/shard_map/all_gather | solution.py:18
  11.6 4.6 copy-start.1
  101.6 74.6 %copy-start.10 = (bf16[2,1,1,256,1152]{4,3,2,1,0:T(8,128)(2,1)S(1)}, bf16[2,1,1,256,1152]{4,3,2,1,0:T(8,128)(2,1)}, u32[]{:S(2)}) copy-start(bf16[2,1,1,256,1152]{4,3,2,1,0:T(8,128)(2,1)} %param.15) | copy-start | bytes 3538948
  192.0 211.2 %all-reduce.3.cloned.1.call-start = ((), (), s32[]{:S(2)}) async-start(), calls=%async_computation | async-start | bytes 2359296 | tf_op jit(solution)/shard_map/psum | solution.py:13
  192.6 499.8 %all-gather.11.cloned.1.call-start = ((), (), s32[]{:S(2)}) async-start(), calls=%async_computation.3 | async-start | bytes 20054016 | tf_op jit(solution)/shard_map/all_gather | solution.py:18
  403.2 30.6 %copy-start = (f32[256,1152]{1,0:T(8,128)S(1)}, f32[256,1152]{1,0:T(8,128)}, u32[]{:S(2)}) copy-start(f32[256,1152]{1,0:T(8,128)} %fusion.18) | copy-start | bytes 3538948
  404.7 28.1 %collective-permute-start.2 = (f32[1,256,1152]{2,1,0:T(8,128)S(1)}, f32[1,256,1152]{2,1,0:T(8,128)S(1)}, u32[]{:S(2)}, u32[]{:S(2)}) collective-permute-start(f32[1,256,1152]{2,1,0:T(8,128)S(1)} %add.160), channel_id=1, source_target_pairs={{8,0},{16,8},{24,16},{32,24},{40,32},{48,40},{56,48},{64,56},{72,6... | collective-permute-start | bytes 3538952 | tf_op jit(solution)/shard_map/ppermute | solution.py:30
  432.8 1.0 copy-start.2
  436.3 28.7 %collective-permute-start.3 = (f32[1,256,1152]{2,1,0:T(8,128)S(1)}, f32[1,256,1152]{2,1,0:T(8,128)S(1)}, u32[]{:S(2)}, u32[]{:S(2)}) collective-permute-start(f32[1,256,1152]{2,1,0:T(8,128)S(1)} %get-tuple-element.107), channel_id=1, source_target_pairs={{16,0},{24,8},{32,16},{40,24},{48,32},{56,40},{64,48},{72,56},{80,... | collective-permute-start | bytes 3538952 | tf_op jit(solution)/shard_map/ppermute | solution.py:30
  437.6 52.7 %collective-permute-start = (f32[1,256,1152]{2,1,0:T(8,128)}, f32[1,256,1152]{2,1,0:T(8,128)S(1)}, u32[]{:S(2)}, u32[]{:S(2)}) collective-permute-start(f32[1,256,1152]{2,1,0:T(8,128)} %get-tuple-element.108), channel_id=1, source_target_pairs={{8,0},{16,8},{24,16},{32,24},{40,32},{48,40},{56,48},{64,56},{72,6... | collective-permute-start | bytes 3538952 | tf_op jit(solution)/shard_map/ppermute | solution.py:30
  465.0 25.3 %copy-start.4 = (f32[1,256,1152]{2,1,0:T(8,128)}, f32[1,256,1152]{2,1,0:T(8,128)S(1)}, u32[]{:S(2)}) copy-start(f32[1,256,1152]{2,1,0:T(8,128)S(1)} %collective-permute-done.3) | copy-start | bytes 3538948
  490.3 1.1 copy-start.5
  493.2 30.8 %collective-permute-start.4 = (f32[1,256,1152]{2,1,0:T(8,128)S(1)}, f32[1,256,1152]{2,1,0:T(8,128)S(1)}, u32[]{:S(2)}, u32[]{:S(2)}) collective-permute-start(f32[1,256,1152]{2,1,0:T(8,128)S(1)} %get-tuple-element.105), channel_id=1, source_target_pairs={{32,0},{40,8},{48,16},{56,24},{64,32},{72,40},{80,48},{88,56},{96,... | collective-permute-start | bytes 3538952 | tf_op jit(solution)/shard_map/ppermute | solution.py:30
  494.5 30.3 %collective-permute-start.1 = (f32[1,256,1152]{2,1,0:T(8,128)S(1)}, f32[1,256,1152]{2,1,0:T(8,128)}, u32[]{:S(2)}, u32[]{:S(2)}) collective-permute-start(f32[1,256,1152]{2,1,0:T(8,128)S(1)} %get-tuple-element.106), channel_id=1, source_target_pairs={{16,0},{24,8},{32,16},{40,24},{48,32},{56,40},{64,48},{72,56},{80,... | collective-permute-start | bytes 3538952 | tf_op jit(solution)/shard_map/ppermute | solution.py:30
  524.1 1.0 copy-start.3
  527.0 1.2 copy-start.7
  527.0 1.6 copy-start.11
  544.5 237.8 %all-reduce.5.cloned.1.call-start = ((), (), s32[]{:S(2)}) async-start(), calls=%async_computation.1 | async-start | bytes 2359296 | tf_op jit(solution)/shard_map/psum | solution.py:13
Sparse Core Ops, SparseCore 0:
  10.3 74.9 all-gather.14
  88.3 71.5 all-gather.12
  192.1 121.1 all-gather.8
  316.5 86.6 all-reduce.2
  544.6 147.7 all-gather.10
  695.6 86.6 all-reduce.4
where the time goes:
time: 794 us; the launch traced here: 792 us
  waiting for transfers between devices  678 us (85%)
  matrix products  40.6 us (5%)
  local copies, waits for them, and re-layouts  35.5 us (4%)
  other arithmetic  15.6 us (2%)
  between operations  15 us (2%)
    all_gather x2, waiting for transfers between devices, carried_in(): gathered = lax.all_gather(part, axis)  268 us
    psum x2, waiting for transfers between devices, spread_2(): return lax.psum(jnp.where(mine, shard, jnp.zeros_like(shard)), axis)  180 us
    ppermute x5, waiting for transfers between devices, from_behind(): return lax.ppermute(shard, axis, pairs)  102 us
    all_gather x1, waiting for transfers between devices, per_device(): lax.all_gather(w_down, ('tm', 'batch'), axis=0, tiled=True)  68 us
    all_gather x1, waiting for transfers between devices, per_device(): lax.all_gather(w_up, ('tm', 'batch'), axis=0, tiled=True)  58.2 us
    unnamed x26, local copies, waits for them, and re-layouts  35.3 us
    dot_general x2, matrix products, dense_pair(): return jnp.dot(activated, down_rows, preferred_element_type=jnp.float32)  31.7 us
  transfers between devices with their start and end apart: 11, of which 11 were waited for; matrix products, arithmetic and copies ran while one was open for 4% of the time, Pallas kernels for 0%

commit v1 on v0

--- a/solution.py
+++ b/solution.py
@@ -10,7 +10,7 @@
 
 def spread_2(shard, axis, root):
     mine = lax.axis_index(axis) == root
-    return lax.psum(jnp.where(mine, shard, jnp.zeros_like(shard)), axis)
+    return jnp.sum(lax.all_gather(jnp.where(mine, shard, jnp.zeros_like(shard)), axis), axis=0)
 
 
 def carried_in(part, axis, combine, identity):

time: 794 us -> 882 us (1.11)
  waiting for transfers between devices: 678 us -> 752 us
  other arithmetic: 15.6 us -> 27.8 us
    all_gather x0 -> x2, waiting for transfers between devices: none -> 214 us  [spread_2(): lax.all_gather(jnp.where(mine, shard, jnp.zeros_like(shard)), axis)]
    psum x2 -> x0, waiting for transfers between devices: 180 us -> none  [spread_2(): return lax.psum(jnp.where(mine, shard, jnp.zeros_like(shard)), axis)]
    ppermute x5, waiting for transfers between devices: 102 us -> 160 us  [from_behind(): return lax.ppermute(shard, axis, pairs)]
    all_gather x2, waiting for transfers between devices: 268 us -> 249 us  [carried_in(): gathered = lax.all_gather(part, axis)]
    reduce_sum x0 -> x2, other arithmetic: none -> 14.7 us  [spread_2(): jnp.sum(lax.all_gather(jnp.where(mine, shard, jnp.zeros_like(shard)), axi...]
    all_gather x1, waiting for transfers between devices: 68 us -> 58.2 us  [per_device(): lax.all_gather(w_down, ('tm', 'batch'), axis=0, tiled=True)]
    all_gather x1, waiting for transfers between devices: 58.2 us -> 67.9 us  [per_device(): lax.all_gather(w_up, ('tm', 'batch'), axis=0, tiled=True)]
    unnamed x26 -> x22, local copies, waits for them, and re-layouts: 35.3 us -> 36.7 us
  transfers between devices with their start and end apart: 11 -> 11, of which waited for: 11 -> 10; matrix products, arithmetic and copies ran while one was open for 4% -> 8% of each run, Pallas kernels for 0% -> 0%
where the time goes in v1:
time: 882 us; the launch traced here: 879 us
  waiting for transfers between devices  752 us (85%)
  matrix products  41 us (5%)
  local copies, waits for them, and re-layouts  36.9 us (4%)
  other arithmetic  27.8 us (3%)
  between operations  15 us (2%)
    all_gather x2, waiting for transfers between devices, carried_in(): gathered = lax.all_gather(part, axis)  249 us
    all_gather x2, waiting for transfers between devices, spread_2(): lax.all_gather(jnp.where(mine, shard, jnp.zeros_like(shard)), axis)  214 us
    ppermute x5, waiting for transfers between devices, from_behind(): return lax.ppermute(shard, axis, pairs)  160 us
    all_gather x1, waiting for transfers between devices, per_device(): lax.all_gather(w_up, ('tm', 'batch'), axis=0, tiled=True)  67.9 us
    all_gather x1, waiting for transfers between devices, per_device(): lax.all_gather(w_down, ('tm', 'batch'), axis=0, tiled=True)  58.2 us
    unnamed x22, local copies, waits for them, and re-layouts  36.7 us
    dot_general x2, matrix products, dense_pair(): return jnp.dot(activated, down_rows, preferred_element_type=jnp.float32)  32 us
  transfers between devices with their start and end apart: 11, of which 10 were waited for; matrix products, arithmetic and copies ran while one was open for 8% of the time, Pallas kernels for 0%

profile of v1, /device:TPU:0, one launch (start us, length us, event | category | flops | bytes accessed | tf_op | source)
XLA Modules:
  0.0 879.0 jit_solution(17988814907854567701)
XLA Ops:
  6.5 0.0 all-gather.20.cloned.1.call-start
  6.5 0.7 all-gather.20.cloned.1.call-update
  7.3 0.0 all-gather.22.cloned.1.call-start
  7.3 0.7 all-gather.22.cloned.1.call-update
  8.0 0.0 all-gather.12.cloned.1.call-start
  8.1 2.4 broadcast_select_fusion.1
  10.4 0.0 copy-start.6
  10.4 0.0 copy-start.7
  10.4 0.0 copy-start.4
  10.4 0.0 all-gather.12.cloned.1.call-update
  10.5 0.0 all-gather.14.cloned.1.call-start
  11.8 0.1 fusion.88
  11.9 0.0 copy-done.6
  11.9 0.0 copy-done.7
  11.9 0.7 select_reduce_fusion
  12.6 0.0 copy-done.4
  12.6 4.5 fusion.74
  17.2 0.0 copy-done
  17.2 0.3 fusion.36
  17.5 67.9 %all-gather.20.cloned.1.call-done = bf16[128,36,1152]{2,1,0:T(8,128)(2,1)} async-done(((bf16[1,36,1152]{2,1,0:T(8,128)(2,1)}), bf16[128,36,1152]{2,1,0:T(8,128)(2,1)}) %all-gather.20.cloned.1.call-update) | async-done | bytes 10616848 | tf_op jit(solution)/shard_map/all_gather | solution.py:80
  85.3 16.3 %reshape.297 = bf16[4608,1152]{1,0:T(8,128)(2,1)} reshape(bf16[128,36,1152]{2,1,0:T(8,128)(2,1)} %all-gather.20.cloned.1.call-done) | data formatting | bytes 21233664
  101.6 58.2 %all-gather.22.cloned.1.call-done = bf16[128,36,1152]{2,1,0:T(8,128)(2,1)} async-done(((bf16[1,36,1152]{2,1,0:T(8,128)(2,1)}), bf16[128,36,1152]{2,1,0:T(8,128)(2,1)}) %all-gather.22.cloned.1.call-update) | async-done | bytes 10616848 | tf_op jit(solution)/shard_map/all_gather | solution.py:81
  159.9 16.5 %reshape.299 = bf16[4608,1152]{1,0:T(8,128)(2,1)} reshape(bf16[128,36,1152]{2,1,0:T(8,128)(2,1)} %all-gather.22.cloned.1.call-done) | data formatting | bytes 21233664
  176.4 0.0 copy-done.8
  176.4 16.2 %fusion.18 = f32[256,1152]{1,0:T(8,128)} fusion(bf16[4608,1152]{1,0:T(8,128)(2,1)} %reshape.299, f32[1,1,256,1152]{3,2,1,0:T(8,128)S(1)} %copy-done, bf16[4608,1152]{1,0:T(8,128)(2,1)} %reshape.297, bf16[2,1,1,256,1152]{4,3,2,1,0:T(8,128)(2,1)S(1)} %copy-done.8, f32[]{:T(128)} %get-tuple-element.86, f32[1152]{0:T(1024)S(1)} %get-tuple-element.82, ...), kind=kOutput, calls=%fused_computation.24 | convolution fusion | flops 5449678848 | bytes 25389064 | tf_op jit(solution)/shard_map/dot_general | solution.py:44
  192.6 0.0 all-gather.14.cloned.1.call-update
  192.6 0.0 all-gather.18.cloned.1.call-start
  192.7 90.6 %all-gather.12.cloned.1.call-done = f32[16,1,256,1152]{3,2,1,0:T(8,128)} async-done(((f32[1,1,256,1152]{3,2,1,0:T(8,128)}), f32[16,1,256,1152]{3,2,1,0:T(8,128)}) %all-gather.12.cloned.1.call-update) | async-done | bytes 18874384 | tf_op jit(solution)/shard_map/all_gather | solution.py:13
  283.3 7.4 reduce_sum.94
  290.6 116.5 %all-gather.14.cloned.1.call-done = f32[4096,1152]{1,0:T(8,128)} async-done(((f32[256,1152]{1,0:T(8,128)}), f32[4096,1152]{1,0:T(8,128)}) %all-gather.14.cloned.1.call-update) | async-done | bytes 18874384 | tf_op jit(solution)/shard_map/all_gather | solution.py:18
  407.1 0.1 broadcast.224.clone
  407.2 0.1 bitcast_add_fusion.4
  407.3 1.3 collective-permute-start.2
  408.6 29.4 %collective-permute-done.2 = f32[1,256,1152]{2,1,0:T(8,128)S(1)} collective-permute-done((f32[1,256,1152]{2,1,0:T(8,128)S(1)}, f32[1,256,1152]{2,1,0:T(8,128)S(1)}, u32[]{:S(2)}, u32[]{:S(2)}) %collective-permute-start.2) | collective-permute-done | bytes 1179680 | tf_op jit(solution)/shard_map/ppermute | solution.py:30
  438.1 1.0 copy-done.1
  439.1 1.8 select_select_fusion.2
  440.9 1.3 collective-permute-start
  442.2 1.3 collective-permute-start.3
  443.5 49.6 %collective-permute-done = f32[1,256,1152]{2,1,0:T(8,128)S(1)} collective-permute-done((f32[1,256,1152]{2,1,0:T(8,128)S(1)}, f32[1,256,1152]{2,1,0:T(8,128)S(1)}, u32[]{:S(2)}, u32[]{:S(2)}) %collective-permute-start) | collective-permute-done | bytes 1179680 | tf_op jit(solution)/shard_map/ppermute | solution.py:30
  493.1 0.0 collective-permute-done.3
  493.1 1.0 copy-done.3
  494.1 2.9 select_select_fusion.1
  497.0 1.3 collective-permute-start.1
  498.3 1.5 collective-permute-start.4
  499.8 0.1 fusion.86
  499.9 4.4 fusion.72
  504.3 0.6 slice_reduce_fusion.1
  504.9 54.6 %collective-permute-done.1 = f32[1,256,1152]{2,1,0:T(8,128)S(1)} collective-permute-done((f32[1,256,1152]{2,1,0:T(8,128)}, f32[1,256,1152]{2,1,0:T(8,128)S(1)}, u32[]{:S(2)}, u32[]{:S(2)}) %collective-permute-start.1) | collective-permute-done | bytes 1179680 | tf_op jit(solution)/shard_map/ppermute | solution.py:30
  559.5 26.4 %collective-permute-done.4 = f32[1,256,1152]{2,1,0:T(8,128)S(1)} collective-permute-done((f32[1,256,1152]{2,1,0:T(8,128)S(1)}, f32[1,256,1152]{2,1,0:T(8,128)S(1)}, u32[]{:S(2)}, u32[]{:S(2)}) %collective-permute-start.4) | collective-permute-done | bytes 1179680 | tf_op jit(solution)/shard_map/ppermute | solution.py:30
  586.0 1.0 copy-done.2
  587.0 2.5 broadcast_select_fusion
  589.5 0.1 reduce_sum.103
  589.7 0.3 multiply_reduce_fusion
  589.9 0.3 copy-done.5
  590.2 0.6 copy-done.9
  590.8 15.8 %fusion.22 = f32[1,256,1152]{2,1,0:T(8,128)} fusion(f32[1,256,1152]{2,1,0:T(8,128)S(1)} %get-tuple-element.104, bf16[4608,1152]{1,0:T(8,128)(2,1)} %reshape.299, bf16[4608,1152]{1,0:T(8,128)(2,1)} %reshape.297, bf16[2,1,1,256,1152]{4,3,2,1,0:T(8,128)(2,1)S(1)} %copy-done.9, f32[]{:T(128)} %get-tuple-element.85, f32[1152]{0:T(1024)S(1)} %copy-done.5, ...), kind=kOutput, calls=%fused_computation.28 | convolution fusion | flops 5449678848 | bytes 25389064 | tf_op jit(solution)/shard_map/dot_general | solution.py:44
  606.6 0.0 all-gather.18.cloned.1.call-update
  606.7 0.0 all-gather.16.cloned.1.call-start
  606.7 0.5 all-gather.16.cloned.1.call-update
  607.2 132.6 %all-gather.18.cloned.1.call-done = f32[16,256,1152]{2,1,0:T(8,128)} async-done(((f32[1,256,1152]{2,1,0:T(8,128)}), f32[16,256,1152]{2,1,0:T(8,128)}) %all-gather.18.cloned.1.call-update) | async-done | bytes 18874384 | tf_op jit(solution)/shard_map/all_gather | solution.py:18
  739.8 0.1 broadcast.224
  739.9 123.7 %all-gather.16.cloned.1.call-done = f32[16,256,1152]{2,1,0:T(8,128)} async-done(((f32[1,256,1152]{2,1,0:T(8,128)}), f32[16,256,1152]{2,1,0:T(8,128)}) %all-gather.16.cloned.1.call-update) | async-done | bytes 18874384 | tf_op jit(solution)/shard_map/all_gather | solution.py:13
  863.6 7.4 reduce.15
  871.0 1.1 fusion.33
  (14 shorter events, 0.1 us)
Async XLA Ops:
  6.5 78.8 %all-gather.20.cloned.1.call-start = ((), (), s32[]{:S(2)}) async-start(), calls=%async_computation.4 | async-start | bytes 11888640 | tf_op jit(solution)/shard_map/all_gather | solution.py:80
  7.3 152.6 %all-gather.22.cloned.1.call-start = ((), (), s32[]{:S(2)}) async-start(), calls=%async_computation.5 | async-start | bytes 11888640 | tf_op jit(solution)/shard_map/all_gather | solution.py:81
  8.0 275.3 %all-gather.12.cloned.1.call-start = ((), (), s32[]{:S(2)}) async-start(), calls=%async_computation | async-start | bytes 20054016 | tf_op jit(solution)/shard_map/all_gather | solution.py:13
  10.4 1.5 copy-start.6
  10.4 1.5 copy-start.7
  10.4 2.2 copy-start.4
  10.5 396.6 %all-gather.14.cloned.1.call-start = ((), (), s32[]{:S(2)}) async-start(), calls=%async_computation.1 | async-start | bytes 20054016 | tf_op jit(solution)/shard_map/all_gather | solution.py:18
  12.6 4.6 copy-start
  101.6 74.8 %copy-start.8 = (bf16[2,1,1,256,1152]{4,3,2,1,0:T(8,128)(2,1)S(1)}, bf16[2,1,1,256,1152]{4,3,2,1,0:T(8,128)(2,1)}, u32[]{:S(2)}) copy-start(bf16[2,1,1,256,1152]{4,3,2,1,0:T(8,128)(2,1)} %param.15) | copy-start | bytes 3538948
  192.6 547.2 %all-gather.18.cloned.1.call-start = ((), (), s32[]{:S(2)}) async-start(), calls=%async_computation.3 | async-start | bytes 20054016 | tf_op jit(solution)/shard_map/all_gather | solution.py:18
  407.3 30.7 %collective-permute-start.2 = (f32[1,256,1152]{2,1,0:T(8,128)S(1)}, f32[1,256,1152]{2,1,0:T(8,128)S(1)}, u32[]{:S(2)}, u32[]{:S(2)}) collective-permute-start(f32[1,256,1152]{2,1,0:T(8,128)S(1)} %bitcast_add_fusion.4), channel_id=1, source_target_pairs={{8,0},{16,8},{24,16},{32,24},{40,32},{48,40},{56,48},{64,56},{72,6... | collective-permute-start | bytes 3538952 | tf_op jit(solution)/shard_map/ppermute | solution.py:30
  438.1 1.0 copy-start.1
  440.9 52.2 %collective-permute-start = (f32[1,256,1152]{2,1,0:T(8,128)S(1)}, f32[1,256,1152]{2,1,0:T(8,128)S(1)}, u32[]{:S(2)}, u32[]{:S(2)}) collective-permute-start(f32[1,256,1152]{2,1,0:T(8,128)S(1)} %get-tuple-element.108), channel_id=1, source_target_pairs={{8,0},{16,8},{24,16},{32,24},{40,32},{48,40},{56,48},{64,56},{72,6... | collective-permute-start | bytes 3538952 | tf_op jit(solution)/shard_map/ppermute | solution.py:30
  442.2 50.9 %collective-permute-start.3 = (f32[1,256,1152]{2,1,0:T(8,128)S(1)}, f32[1,256,1152]{2,1,0:T(8,128)}, u32[]{:S(2)}, u32[]{:S(2)}) collective-permute-start(f32[1,256,1152]{2,1,0:T(8,128)S(1)} %get-tuple-element.107), channel_id=1, source_target_pairs={{16,0},{24,8},{32,16},{40,24},{48,32},{56,40},{64,48},{72,56},{80,... | collective-permute-start | bytes 3538952 | tf_op jit(solution)/shard_map/ppermute | solution.py:30
  493.1 1.0 copy-start.3
  497.0 62.6 %collective-permute-start.1 = (f32[1,256,1152]{2,1,0:T(8,128)}, f32[1,256,1152]{2,1,0:T(8,128)S(1)}, u32[]{:S(2)}, u32[]{:S(2)}) collective-permute-start(f32[1,256,1152]{2,1,0:T(8,128)} %get-tuple-element.106), channel_id=1, source_target_pairs={{16,0},{24,8},{32,16},{40,24},{48,32},{56,40},{64,48},{72,56},{80,... | collective-permute-start | bytes 3538952 | tf_op jit(solution)/shard_map/ppermute | solution.py:30
  498.3 87.7 %collective-permute-start.4 = (f32[1,256,1152]{2,1,0:T(8,128)S(1)}, f32[1,256,1152]{2,1,0:T(8,128)S(1)}, u32[]{:S(2)}, u32[]{:S(2)}) collective-permute-start(f32[1,256,1152]{2,1,0:T(8,128)S(1)} %get-tuple-element.105), channel_id=1, source_target_pairs={{32,0},{40,8},{48,16},{56,24},{64,32},{72,40},{80,48},{88,56},{96,... | collective-permute-start | bytes 3538952 | tf_op jit(solution)/shard_map/ppermute | solution.py:30
  586.0 1.0 copy-start.2
  589.5 0.7 copy-start.5
  589.5 1.3 copy-start.9
  606.7 257.0 %all-gather.16.cloned.1.call-start = ((), (), s32[]{:S(2)}) async-start(), calls=%async_computation.2 | async-start | bytes 20054016 | tf_op jit(solution)/shard_map/all_gather | solution.py:13
Sparse Core Ops, SparseCore 0:
  10.3 74.9 all-gather.19
  88.3 71.5 all-gather.21
  162.1 121.1 all-gather.11
  285.3 121.7 all-gather.13
  606.8 132.9 all-gather.17
  741.8 121.7 all-gather.15
